TPU v7x, 512 devices: a whole 4x4x16 slice. The times are simulated.
512 devices in a mesh: grp: 64 (over z, x_lo, core), freq: 8 (over y, x_hi).
Axes of the slice: x: 4 (x_hi: 2, x_lo: 2; x = x_hi * 2 + x_lo), y: 4, z: 16, core: 2. Of those that a mesh axis runs over, the one named last changes fastest.
Arguments:
- spectra: bfloat16 [8192, 8, 2, 1024], P('grp', None, None, 'freq')
- pairing: int32 [2, 64], replicated, may hold values from 0 to 63, as said below
Outputs:
- correlations: float32 [2, 4096, 128, 256], P(None, ('grp', 'freq'))
Inputs may be any that keep to these rules, and one draw needn't show every extreme that they name: In every round each group's partner is another group, and pairing[r, pairing[r, g]] = g.
All inputs are finite; a program needn't handle non-finite values.
Results may differ from a plain program's by a relative error of at most 0.0055.
Values may be sent and summed in bfloat16 or wider, within the bound.
A program may use at most 64 MiB of HBM per device.

v0:
```python
import math
import jax
import jax.numpy as jnp
from jax import lax
from jax.sharding import PartitionSpec as P

LAGS = 256
VIRTUAL_SOURCES = 64
ROUNDS = 2


def lag_table(bin_count, freq_total):
    bins = jnp.arange(bin_count, dtype=jnp.int32)
    shifts = jnp.arange(LAGS, dtype=jnp.int32) - LAGS // 2
    phase_int = bins[:, None] * shifts[None, :] % (2 * freq_total)
    theta = phase_int.astype(jnp.float32) * (math.pi / freq_total)
    weights = jnp.where(bins == 0, 1.0, 2.0).astype(jnp.float32) / (2.0 * freq_total)
    return jnp.stack(
        [weights[:, None] * jnp.cos(theta), -weights[:, None] * jnp.sin(theta)]
    ).astype(jnp.bfloat16)


def cross_spectra(source_channels, partner):
    src_count, win_count, two_parts, bins = source_channels.shape
    real_left = source_channels.reshape(src_count, win_count * 2, bins)
    imag_left = jnp.stack([source_channels[:, :, 1], -source_channels[:, :, 0]], axis=2).reshape(
        src_count, win_count * 2, bins
    )
    right = partner.reshape(partner.shape[0], win_count * 2, bins)
    real_part = (
        jnp.einsum("skf,ckf->scf", real_left, right, preferred_element_type=jnp.float32) / win_count
    ).astype(jnp.bfloat16)
    imag_part = (
        jnp.einsum("skf,ckf->scf", imag_left, right, preferred_element_type=jnp.float32) / win_count
    ).astype(jnp.bfloat16)
    return jnp.stack([real_part, imag_part], axis=2)


def per_device(spectra, pairing):
    channel_total, win_count, two_parts, freq_local = spectra.shape
    freq_total = freq_local * lax.axis_size("freq")
    group_count = lax.axis_size("grp")
    per_slot = channel_total // group_count
    energy = lax.psum(jnp.sum(jnp.square(spectra.astype(jnp.float32)), axis=(1, 2, 3)), "freq")
    scaling = lax.rsqrt(energy / (win_count * 2 * freq_total) + 1e-06)
    whitened_spectra = (spectra * scaling[:, None, None, None]).astype(jnp.bfloat16)
    spread = lax.all_to_all(
        whitened_spectra.reshape(group_count, per_slot, win_count, two_parts, freq_local),
        "grp",
        split_axis=0,
        concat_axis=0,
        tiled=True,
    )
    source_channels = whitened_spectra[:: channel_total // VIRTUAL_SOURCES]
    shape_back = (channel_total, win_count, two_parts, freq_local)
    partners = []
    for which_round in range(ROUNDS):
        slots = jnp.take(spread, pairing[which_round], axis=0)
        arrived = lax.all_to_all(slots, "grp", split_axis=0, concat_axis=0, tiled=True)
        partners.append(arrived.reshape(shape_back))
    whole_table = lag_table(freq_total, freq_total)
    results = []
    for which_round in range(ROUNDS):
        spectrum = cross_spectra(source_channels, partners[which_round])
        results.append(
            jnp.einsum(
                "scpf,pfl->scl",
                lax.all_to_all(spectrum, "freq", split_axis=0, concat_axis=3, tiled=True),
                whole_table,
                preferred_element_type=jnp.float32,
            )
        )
    return jnp.stack(results)


def solution(mesh):
    placed = (P("grp", None, None, "freq"), P())
    return jax.shard_map(
        per_device,
        mesh=mesh,
        in_specs=placed,
        out_specs=P(None, ("grp", "freq"), None, None),
        check_vma=False,
    )
```

profile of v0, /device:TPU:32, one launch (start us, length us, event | category | flops | bytes accessed | tf_op | source)
XLA Modules:
  0.0 286.4 jit_solution(10637405546343010891)
XLA Ops:
  0.0 2.1 fusion.4
  2.1 24.5 %psum.7 = f32[128]{0:T(128)S(1)} all-reduce(f32[128]{0:T(128)S(1)} %fusion.4), channel_id=1, replica_groups=mesh['grp'=64,'freq'=8] {'freq'}, use_global_device_ids=true, to_apply=%region_1.0 | all-reduce | flops 128 | bytes 1024 | tf_op jit(solution)/shard_map/psum | solution.py:44
  26.6 1.5 fusion.5
  28.1 0.9 copy.18
  29.0 15.8 %all-to-all-start = ((bf16[64,2,8,2,128]{4,2,3,1,0:T(8,128)(2,1)}), bf16[64,2,8,2,128]{4,2,3,1,0:T(8,128)(2,1)S(1)}, u32[]{:S(2)}, u32[]{:S(2)}) async-start(bf16[64,2,8,2,128]{4,2,3,1,0:T(8,128)(2,1)} %bitcast.1), calls=%async_computation | async-start | bytes 1048576 | tf_op jit(solution)/shard_map/all_to_all | solution.py:47
  44.8 0.8 compare_and_fusion.1
  45.6 31.9 %all-to-all-done = bf16[64,2,8,2,128]{4,2,3,1,0:T(8,128)(2,1)S(1)} async-done(((bf16[64,2,8,2,128]{4,2,3,1,0:T(8,128)(2,1)}), bf16[64,2,8,2,128]{4,2,3,1,0:T(8,128)(2,1)S(1)}, u32[]{:S(2)}, u32[]{:S(2)}) %all-to-all-start) | async-done | bytes 524320 | tf_op jit(solution)/shard_map/all_to_all | solution.py:47
  77.4 0.7 gather_fusion
  78.1 0.9 broadcast_select_fusion.1
  79.0 5.6 %all-to-all-start.1 = ((bf16[64,2,8,2,128]{4,2,3,1,0:T(8,128)(2,1)}), bf16[64,2,8,2,128]{4,2,3,1,0:T(8,128)(2,1)S(1)}, u32[]{:S(2)}, u32[]{:S(2)}) async-start(bf16[64,2,8,2,128]{4,2,3,1,0:T(8,128)(2,1)} %broadcast_select_fusion.1), calls=%async_computation.1 | async-start | bytes 1048576 | tf_op jit(solution)/shard_map/all_to_all | solution.py:59
  84.6 0.7 gather_fusion.1
  85.3 0.9 broadcast_select_fusion
  86.2 31.1 %all-to-all-done.1 = bf16[64,2,8,2,128]{4,2,3,1,0:T(8,128)(2,1)S(1)} async-done(((bf16[64,2,8,2,128]{4,2,3,1,0:T(8,128)(2,1)}), bf16[64,2,8,2,128]{4,2,3,1,0:T(8,128)(2,1)S(1)}, u32[]{:S(2)}, u32[]{:S(2)}) %all-to-all-start.1) | async-done | bytes 524320 | tf_op jit(solution)/shard_map/all_to_all | solution.py:59
  117.3 5.6 %all-to-all-start.3 = ((bf16[64,2,8,2,128]{4,2,3,1,0:T(8,128)(2,1)}), bf16[64,2,8,2,128]{4,2,3,1,0:T(8,128)(2,1)S(1)}, u32[]{:S(2)}, u32[]{:S(2)}) async-start(bf16[64,2,8,2,128]{4,2,3,1,0:T(8,128)(2,1)} %broadcast_select_fusion), calls=%async_computation.3 | async-start | bytes 1048576 | tf_op jit(solution)/shard_map/all_to_all | solution.py:59
  123.0 0.2 slice.18
  123.2 0.6 copy.20
  123.7 0.5 fusion.15
  124.2 0.6 pad_maximum_fusion.3
  124.8 0.6 copy.22
  125.4 0.4 copy.19
  125.8 0.7 copy.21
  126.5 0.8 fusion.1
  127.3 0.8 fusion
  128.1 0.4 pad_maximum_fusion
  128.5 4.6 %copy.24 = bf16[64,128,2,128]{1,3,2,0:T(8,128)(2,1)} copy(bf16[64,128,2,128]{1,0,3,2:T(8,128)(2,1)S(1)} %pad_maximum_fusion) | data formatting | bytes 8388608 | tf_op jit(solution)/shard_map/stack | solution.py:36
  133.2 22.5 %all-to-all-done.3 = bf16[64,2,8,2,128]{4,2,3,1,0:T(8,128)(2,1)S(1)} async-done(((bf16[64,2,8,2,128]{4,2,3,1,0:T(8,128)(2,1)}), bf16[64,2,8,2,128]{4,2,3,1,0:T(8,128)(2,1)S(1)}, u32[]{:S(2)}, u32[]{:S(2)}) %all-to-all-start.3) | async-done | bytes 524320 | tf_op jit(solution)/shard_map/all_to_all | solution.py:59
  155.7 4.8 %all-to-all-start.2 = ((bf16[64,128,2,128]{1,3,2,0:T(8,128)(2,1)}), bf16[64,128,2,128]{1,3,2,0:T(8,128)(2,1)}, u32[]{:S(2)}, u32[]{:S(2)}) async-start(bf16[64,128,2,128]{1,3,2,0:T(8,128)(2,1)} %copy.24), calls=%async_computation.2 | async-start | bytes 8388608 | tf_op jit(solution)/shard_map/all_to_all | solution.py:68
  160.5 0.4 copy.26
  160.9 0.7 copy.27
  161.7 0.8 fusion.3
  162.4 0.8 fusion.2
  163.2 0.4 pad_maximum_fusion.1
  163.6 4.7 %copy.29 = bf16[64,128,2,128]{1,3,2,0:T(8,128)(2,1)} copy(bf16[64,128,2,128]{1,0,3,2:T(8,128)(2,1)S(1)} %pad_maximum_fusion.1) | data formatting | bytes 8388608 | tf_op jit(solution)/shard_map/stack | solution.py:36
  168.3 43.0 %all-to-all-done.2 = bf16[64,128,2,128]{1,3,2,0:T(8,128)(2,1)} async-done(((bf16[64,128,2,128]{1,3,2,0:T(8,128)(2,1)}), bf16[64,128,2,128]{1,3,2,0:T(8,128)(2,1)}, u32[]{:S(2)}, u32[]{:S(2)}) %all-to-all-start.2) | async-done | bytes 4194336 | tf_op jit(solution)/shard_map/all_to_all | solution.py:68
  211.4 4.6 %all-to-all-start.4 = ((bf16[64,128,2,128]{1,3,2,0:T(8,128)(2,1)}), bf16[64,128,2,128]{1,3,2,0:T(8,128)(2,1)}, u32[]{:S(2)}, u32[]{:S(2)}) async-start(bf16[64,128,2,128]{1,3,2,0:T(8,128)(2,1)} %copy.29), calls=%async_computation.4 | async-start | bytes 8388608 | tf_op jit(solution)/shard_map/all_to_all | solution.py:68
  215.9 4.6 %multiply_convert_fusion.5 = (bf16[1,1024,256]{2,1,0:T(8,128)(2,1)S(1)}, bf16[1,1024,256]{2,1,0:T(8,128)(2,1)S(1)}) fusion(s32[256]{0:T(256)S(1)} %iota_add_fusion, f32[1024]{0:T(1024)S(1)} %get-tuple-element.16, f32[1024]{0:T(1024)S(1)} %get-tuple-element.17), kind=kLoop, calls=%fused_computation.27 | loop fusion | flops 4718592 | bytes 1057792 | tf_op jit(solution)/shard_map/convert
  220.5 6.8 %copy.25 = bf16[8,8,128,2,128]{4,0,2,3,1:T(8,128)(2,1)} copy(bf16[8,8,128,2,128]{2,4,3,1,0:T(8,128)(2,1)} %bitcast.9) | data formatting | bytes 8388608 | tf_op jit(solution)/shard_map/all_to_all | solution.py:68
  227.3 7.3 %all_to_all.40 = bf16[8,128,2,1024]{3,1,2,0:T(8,128)(2,1)} reshape(bf16[8,128,2,8,128]{4,3,1,2,0:T(8,128)(2,1)} %bitcast.61) | data formatting | bytes 8388608 | tf_op jit(solution)/shard_map/all_to_all | solution.py:68
  234.6 31.5 %all-to-all-done.4 = bf16[64,128,2,128]{1,3,2,0:T(8,128)(2,1)} async-done(((bf16[64,128,2,128]{1,3,2,0:T(8,128)(2,1)}), bf16[64,128,2,128]{1,3,2,0:T(8,128)(2,1)}, u32[]{:S(2)}, u32[]{:S(2)}) %all-to-all-start.4) | async-done | bytes 4194336 | tf_op jit(solution)/shard_map/all_to_all | solution.py:68
  266.0 6.8 %copy.30 = bf16[8,8,128,2,128]{4,0,2,3,1:T(8,128)(2,1)} copy(bf16[8,8,128,2,128]{2,4,3,1,0:T(8,128)(2,1)} %bitcast.21) | data formatting | bytes 8388608 | tf_op jit(solution)/shard_map/all_to_all | solution.py:68
  272.8 7.3 %all_to_all.45 = bf16[8,128,2,1024]{3,1,2,0:T(8,128)(2,1)} reshape(bf16[8,128,2,8,128]{4,3,1,2,0:T(8,128)(2,1)} %bitcast.62) | data formatting | bytes 8388608 | tf_op jit(solution)/shard_map/all_to_all | solution.py:68
  280.1 0.0 copy-start
  280.1 3.6 %convolution_bitcast_fusion.1 = f32[1,8,128,256]{3,2,1,0:T(8,128)S(1)} fusion(bf16[8,128,2,1024]{3,1,2,0:T(8,128)(2,1)} %all_to_all.40, bf16[1,1024,256]{2,1,0:T(8,128)(2,1)S(1)} %get-tuple-element.15, bf16[1,1024,256]{2,1,0:T(8,128)(2,1)S(1)} %get-tuple-element.14), kind=kOutput, calls=%fused_computation.17 | convolution fusion | flops 1074266112 | bytes 6291456 | tf_op jit(solution)/shard_map/scpf,pfl->scl/dot_general | solution.py:66
  283.7 0.0 copy-done
  283.7 1.3 convolution_bitcast_fusion
  285.0 1.5 pad_maximum_fusion.2
  (5 shorter events, 0.0 us)
Async XLA Ops:
  29.0 48.4 %all-to-all-start = ((bf16[64,2,8,2,128]{4,2,3,1,0:T(8,128)(2,1)}), bf16[64,2,8,2,128]{4,2,3,1,0:T(8,128)(2,1)S(1)}, u32[]{:S(2)}, u32[]{:S(2)}) async-start(bf16[64,2,8,2,128]{4,2,3,1,0:T(8,128)(2,1)} %bitcast.1), calls=%async_computation | async-start | bytes 1048576 | tf_op jit(solution)/shard_map/all_to_all | solution.py:47
  79.0 38.3 %all-to-all-start.1 = ((bf16[64,2,8,2,128]{4,2,3,1,0:T(8,128)(2,1)}), bf16[64,2,8,2,128]{4,2,3,1,0:T(8,128)(2,1)S(1)}, u32[]{:S(2)}, u32[]{:S(2)}) async-start(bf16[64,2,8,2,128]{4,2,3,1,0:T(8,128)(2,1)} %broadcast_select_fusion.1), calls=%async_computation.1 | async-start | bytes 1048576 | tf_op jit(solution)/shard_map/all_to_all | solution.py:59
  117.3 38.3 %all-to-all-start.3 = ((bf16[64,2,8,2,128]{4,2,3,1,0:T(8,128)(2,1)}), bf16[64,2,8,2,128]{4,2,3,1,0:T(8,128)(2,1)S(1)}, u32[]{:S(2)}, u32[]{:S(2)}) async-start(bf16[64,2,8,2,128]{4,2,3,1,0:T(8,128)(2,1)} %broadcast_select_fusion), calls=%async_computation.3 | async-start | bytes 1048576 | tf_op jit(solution)/shard_map/all_to_all | solution.py:59
  155.7 55.7 %all-to-all-start.2 = ((bf16[64,128,2,128]{1,3,2,0:T(8,128)(2,1)}), bf16[64,128,2,128]{1,3,2,0:T(8,128)(2,1)}, u32[]{:S(2)}, u32[]{:S(2)}) async-start(bf16[64,128,2,128]{1,3,2,0:T(8,128)(2,1)} %copy.24), calls=%async_computation.2 | async-start | bytes 8388608 | tf_op jit(solution)/shard_map/all_to_all | solution.py:68
  211.4 54.7 %all-to-all-start.4 = ((bf16[64,128,2,128]{1,3,2,0:T(8,128)(2,1)}), bf16[64,128,2,128]{1,3,2,0:T(8,128)(2,1)}, u32[]{:S(2)}, u32[]{:S(2)}) async-start(bf16[64,128,2,128]{1,3,2,0:T(8,128)(2,1)} %copy.29), calls=%async_computation.4 | async-start | bytes 8388608 | tf_op jit(solution)/shard_map/all_to_all | solution.py:68
  280.1 3.6 %copy-start = (bf16[8,128,2,1024]{3,1,2,0:T(8,128)(2,1)S(1)}, bf16[8,128,2,1024]{3,1,2,0:T(8,128)(2,1)}, u32[]{:S(2)}) copy-start(bf16[8,128,2,1024]{3,1,2,0:T(8,128)(2,1)} %all_to_all.45) | copy-start | bytes 12582916
where the time goes:
time: 288 us; the launch traced here: 286 us
  waiting for transfers between devices  160 us (56%)
  local copies, waits for them, and re-layouts  43.2 us (15%)
  starting transfers between devices  36.4 us (13%)
  blocking collectives  24.5 us (9%)
  other arithmetic  14.2 us (5%)
  matrix products  7.98 us (3%)
    all_to_all x2, waiting for transfers between devices, per_device(): lax.all_to_all(spectrum, 'freq', split_axis=0, concat_axis=3, tiled=True)  74.5 us
    all_to_all x2, waiting for transfers between devices, per_device(): lax.all_to_all(slots, 'grp', split_axis=0, concat_axis=0, tiled=True)  53.6 us
    all_to_all x1, waiting for transfers between devices, per_device(): lax.all_to_all(whitened_spectra.reshape(group_count, per_slot, win_count,...  31.9 us
    all_to_all x4, local copies, waits for them, and re-layouts, per_device(): lax.all_to_all(spectrum, 'freq', split_axis=0, concat_axis=3, tiled=True)  28.1 us
    psum x1, blocking collectives, per_device(): lax.psum(jnp.sum(jnp.square(spectra.astype(jnp.float32)), axis=(1, 2, 3))...  24.5 us
    all_to_all x1, starting transfers between devices, per_device(): lax.all_to_all(whitened_spectra.reshape(group_count, per_slot, win_count,...  15.8 us
    all_to_all x2, starting transfers between devices, per_device(): lax.all_to_all(slots, 'grp', split_axis=0, concat_axis=0, tiled=True)  11.2 us
    all_to_all x2, starting transfers between devices, per_device(): lax.all_to_all(spectrum, 'freq', split_axis=0, concat_axis=3, tiled=True)  9.37 us
  transfers between devices with their start and end apart: 5, of which 5 were waited for; matrix products, arithmetic and copies ran while one was open for 11% of the time, Pallas kernels for 0%

commit v1 on v0

--- a/solution.py
+++ b/solution.py
@@ -65,7 +65,12 @@
         results.append(
             jnp.einsum(
                 "scpf,pfl->scl",
-                lax.all_to_all(spectrum, "freq", split_axis=0, concat_axis=3, tiled=True),
+                jnp.concatenate(
+                    lax.all_to_all(
+                        jnp.stack(jnp.split(spectrum, lax.axis_size("freq"), axis=0)), "freq", 0, 0
+                    ),
+                    axis=3,
+                ),
                 whole_table,
                 preferred_element_type=jnp.float32,
             )

time: 288 us -> 274 us (0.951)
  local copies, waits for them, and re-layouts: 43.2 us -> 14.5 us
  other arithmetic: 14.2 us -> 28.5 us
  waiting for transfers between devices: 160 us -> 164 us
    all_to_all x4 -> x0, local copies, waits for them, and re-layouts: 28.1 us -> none  [per_device(): lax.all_to_all(spectrum, 'freq', split_axis=0, concat_axis=3, tiled=True)]
    unnamed x0 -> x14, other arithmetic: none -> 13.1 us
    another operation x2 -> x0, local copies, waits for them, and re-layouts: 9.32 us -> none  [cross_spectra(): return jnp.stack([real_part, imag_part], axis=2)]
    reshape x0 -> x2, local copies, waits for them, and re-layouts: none -> 8.69 us  [per_device(): jnp.concatenate(lax.all_to_all(jnp.stack(jnp.split(spectrum, lax.axis_siz...]
    all_to_all x2, waiting for transfers between devices: 74.5 us -> 80.8 us  [per_device(): lax.all_to_all(jnp.stack(jnp.split(spectrum, lax.axis_size('freq'), axis=...]
  transfers between devices with their start and end apart: 5 -> 5, of which waited for: 5 -> 5; matrix products, arithmetic and copies ran while one was open for 11% -> 13% of each run, Pallas kernels for 0% -> 0%
where the time goes in v1:
time: 274 us
  waiting for transfers between devices  164 us (60%)
  starting transfers between devices  36.3 us (13%)
  other arithmetic  28.5 us (10%)
  blocking collectives  24.5 us (9%)
  local copies, waits for them, and re-layouts  14.5 us (5%)
  matrix products  5.71 us (2%)
    all_to_all x2, waiting for transfers between devices, per_device(): lax.all_to_all(jnp.stack(jnp.split(spectrum, lax.axis_size('freq'), axis=...  80.8 us
    all_to_all x2, waiting for transfers between devices, per_device(): lax.all_to_all(slots, 'grp', split_axis=0, concat_axis=0, tiled=True)  51.1 us
    all_to_all x1, waiting for transfers between devices, per_device(): lax.all_to_all(whitened_spectra.reshape(group_count, per_slot, win_count,...  31.9 us
    psum x1, blocking collectives, per_device(): lax.psum(jnp.sum(jnp.square(spectra.astype(jnp.float32)), axis=(1, 2, 3))...  24.5 us
    all_to_all x1, starting transfers between devices, per_device(): lax.all_to_all(whitened_spectra.reshape(group_count, per_slot, win_count,...  15.8 us
    unnamed x14, other arithmetic  13.1 us
    all_to_all x2, starting transfers between devices, per_device(): lax.all_to_all(slots, 'grp', split_axis=0, concat_axis=0, tiled=True)  11.2 us
    all_to_all x2, starting transfers between devices, per_device(): lax.all_to_all(jnp.stack(jnp.split(spectrum, lax.axis_size('freq'), axis=...  9.3 us
  transfers between devices with their start and end apart: 5, of which 5 were waited for; matrix products, arithmetic and copies ran while one was open for 13% of the time, Pallas kernels for 0%

profile of v1, /device:TPU:32, one launch (start us, length us, event | category | flops | bytes accessed | tf_op | source)
XLA Modules:
  0.0 273.5 jit_solution(16263813167153066676)
XLA Ops:
  0.0 2.1 fusion.4
  2.1 24.5 %psum.7 = f32[128]{0:T(128)S(1)} all-reduce(f32[128]{0:T(128)S(1)} %fusion.4), channel_id=1, replica_groups=mesh['grp'=64,'freq'=8] {'freq'}, use_global_device_ids=true, to_apply=%region_1.0 | all-reduce | flops 128 | bytes 1024 | tf_op jit(solution)/shard_map/psum | solution.py:44
  26.6 1.5 fusion.5
  28.1 0.9 copy.5
  29.0 15.8 %all-to-all-start = ((bf16[64,2,8,2,128]{4,2,3,1,0:T(8,128)(2,1)}), bf16[64,2,8,2,128]{4,2,3,1,0:T(8,128)(2,1)S(1)}, u32[]{:S(2)}, u32[]{:S(2)}) async-start(bf16[64,2,8,2,128]{4,2,3,1,0:T(8,128)(2,1)} %bitcast.1), calls=%async_computation | async-start | bytes 1048576 | tf_op jit(solution)/shard_map/all_to_all | solution.py:47
  44.8 0.8 compare_and_fusion.1
  45.6 31.9 %all-to-all-done = bf16[64,2,8,2,128]{4,2,3,1,0:T(8,128)(2,1)S(1)} async-done(((bf16[64,2,8,2,128]{4,2,3,1,0:T(8,128)(2,1)}), bf16[64,2,8,2,128]{4,2,3,1,0:T(8,128)(2,1)S(1)}, u32[]{:S(2)}, u32[]{:S(2)}) %all-to-all-start) | async-done | bytes 524320 | tf_op jit(solution)/shard_map/all_to_all | solution.py:47
  77.4 0.7 gather_fusion
  78.1 0.9 broadcast_select_fusion.1
  79.0 5.6 %all-to-all-start.1 = ((bf16[64,2,8,2,128]{4,2,3,1,0:T(8,128)(2,1)}), bf16[64,2,8,2,128]{4,2,3,1,0:T(8,128)(2,1)S(1)}, u32[]{:S(2)}, u32[]{:S(2)}) async-start(bf16[64,2,8,2,128]{4,2,3,1,0:T(8,128)(2,1)} %broadcast_select_fusion.1), calls=%async_computation.1 | async-start | bytes 1048576 | tf_op jit(solution)/shard_map/all_to_all | solution.py:59
  84.6 0.7 gather_fusion.1
  85.3 0.9 broadcast_select_fusion
  86.2 31.1 %all-to-all-done.1 = bf16[64,2,8,2,128]{4,2,3,1,0:T(8,128)(2,1)S(1)} async-done(((bf16[64,2,8,2,128]{4,2,3,1,0:T(8,128)(2,1)}), bf16[64,2,8,2,128]{4,2,3,1,0:T(8,128)(2,1)S(1)}, u32[]{:S(2)}, u32[]{:S(2)}) %all-to-all-start.1) | async-done | bytes 524320 | tf_op jit(solution)/shard_map/all_to_all | solution.py:59
  117.3 5.6 %all-to-all-start.3 = ((bf16[64,2,8,2,128]{4,2,3,1,0:T(8,128)(2,1)}), bf16[64,2,8,2,128]{4,2,3,1,0:T(8,128)(2,1)S(1)}, u32[]{:S(2)}, u32[]{:S(2)}) async-start(bf16[64,2,8,2,128]{4,2,3,1,0:T(8,128)(2,1)} %broadcast_select_fusion), calls=%async_computation.3 | async-start | bytes 1048576 | tf_op jit(solution)/shard_map/all_to_all | solution.py:59
  124.2 0.6 pad_maximum_fusion.3
  125.8 0.7 copy.8
  126.5 0.8 fusion.1
  127.3 0.8 fusion
  128.1 0.9 bitcast_dynamic-update-slice_fusion.13
  129.1 0.9 bitcast_dynamic-update-slice_fusion.12
  130.0 1.0 bitcast_dynamic-update-slice_fusion.11
  131.0 0.9 bitcast_dynamic-update-slice_fusion.10
  131.9 1.0 bitcast_dynamic-update-slice_fusion.9
  132.8 0.9 bitcast_dynamic-update-slice_fusion.8
  133.8 0.9 bitcast_dynamic-update-slice_fusion.7
  134.7 1.0 fusion.29
  135.7 20.0 %all-to-all-done.3 = bf16[64,2,8,2,128]{4,2,3,1,0:T(8,128)(2,1)S(1)} async-done(((bf16[64,2,8,2,128]{4,2,3,1,0:T(8,128)(2,1)}), bf16[64,2,8,2,128]{4,2,3,1,0:T(8,128)(2,1)S(1)}, u32[]{:S(2)}, u32[]{:S(2)}) %all-to-all-start.3) | async-done | bytes 524320 | tf_op jit(solution)/shard_map/all_to_all | solution.py:59
  155.7 4.7 %all-to-all-start.2 = ((bf16[8,8,128,2,128]{2,1,4,3,0:T(8,128)(2,1)}), bf16[8,8,128,2,128]{2,1,4,3,0:T(8,128)(2,1)}, u32[]{:S(2)}, u32[]{:S(2)}) async-start(bf16[8,8,128,2,128]{2,1,4,3,0:T(8,128)(2,1)} %fusion.29), calls=%async_computation.2 | async-start | bytes 8388608 | tf_op jit(solution)/shard_map/all_to_all | solution.py:69
  160.8 0.7 copy.14
  161.6 0.8 fusion.3
  162.4 0.8 fusion.2
  163.2 1.0 bitcast_dynamic-update-slice_fusion.6
  164.1 1.0 bitcast_dynamic-update-slice_fusion.5
  165.1 0.9 bitcast_dynamic-update-slice_fusion.4
  166.0 0.9 bitcast_dynamic-update-slice_fusion.3
  166.9 0.9 bitcast_dynamic-update-slice_fusion.2
  167.9 0.9 bitcast_dynamic-update-slice_fusion.1
  168.8 0.9 bitcast_dynamic-update-slice_fusion
  169.7 0.9 fusion.27
  170.7 40.6 %all-to-all-done.2 = bf16[8,8,128,2,128]{2,1,4,3,0:T(8,128)(2,1)} async-done(((bf16[8,8,128,2,128]{2,1,4,3,0:T(8,128)(2,1)}), bf16[8,8,128,2,128]{2,1,4,3,0:T(8,128)(2,1)}, u32[]{:S(2)}, u32[]{:S(2)}) %all-to-all-start.2) | async-done | bytes 4194336 | tf_op jit(solution)/shard_map/all_to_all | solution.py:69
  211.3 4.6 %all-to-all-start.4 = ((bf16[8,8,128,2,128]{2,1,4,3,0:T(8,128)(2,1)}), bf16[8,8,128,2,128]{2,1,4,3,0:T(8,128)(2,1)}, u32[]{:S(2)}, u32[]{:S(2)}) async-start(bf16[8,8,128,2,128]{2,1,4,3,0:T(8,128)(2,1)} %fusion.27), calls=%async_computation.4 | async-start | bytes 8388608 | tf_op jit(solution)/shard_map/all_to_all | solution.py:69
  215.9 4.6 %multiply_convert_fusion.5 = (bf16[1,1024,256]{2,1,0:T(8,128)(2,1)S(1)}, bf16[1,1024,256]{2,1,0:T(8,128)(2,1)S(1)}) fusion(s32[256]{0:T(256)S(1)} %iota_add_fusion, f32[1024]{0:T(1024)S(1)} %get-tuple-element.16, f32[1024]{0:T(1024)S(1)} %get-tuple-element.17), kind=kLoop, calls=%fused_computation.53 | loop fusion | flops 4718592 | bytes 1057792 | tf_op jit(solution)/shard_map/convert
  220.5 5.3 %copy.11 = bf16[8,128,2,8,128]{1,4,3,2,0:T(8,128)(2,1)} copy(bf16[8,128,2,8,128]{1,0,4,2,3:T(8,128)(2,1)} %bitcast.17) | data formatting | bytes 8388608 | tf_op jit(solution)/shard_map/reshape | solution.py:68
  225.8 40.2 %all-to-all-done.4 = bf16[8,8,128,2,128]{2,1,4,3,0:T(8,128)(2,1)} async-done(((bf16[8,8,128,2,128]{2,1,4,3,0:T(8,128)(2,1)}), bf16[8,8,128,2,128]{2,1,4,3,0:T(8,128)(2,1)}, u32[]{:S(2)}, u32[]{:S(2)}) %all-to-all-start.4) | async-done | bytes 4194336 | tf_op jit(solution)/shard_map/all_to_all | solution.py:69
  266.0 3.4 %copy.16 = bf16[8,128,2,8,128]{1,4,3,2,0:T(8,128)(2,1)S(1)} copy(bf16[8,128,2,8,128]{1,0,4,2,3:T(8,128)(2,1)} %bitcast.37) | data formatting | bytes 8388608 | tf_op jit(solution)/shard_map/reshape | solution.py:68
  269.4 1.3 convolution_bitcast_fusion.1
  270.7 1.3 convolution_bitcast_fusion
  272.0 1.5 pad_maximum_fusion
  (13 shorter events, 2.6 us)
Async XLA Ops:
  29.0 48.4 %all-to-all-start = ((bf16[64,2,8,2,128]{4,2,3,1,0:T(8,128)(2,1)}), bf16[64,2,8,2,128]{4,2,3,1,0:T(8,128)(2,1)S(1)}, u32[]{:S(2)}, u32[]{:S(2)}) async-start(bf16[64,2,8,2,128]{4,2,3,1,0:T(8,128)(2,1)} %bitcast.1), calls=%async_computation | async-start | bytes 1048576 | tf_op jit(solution)/shard_map/all_to_all | solution.py:47
  79.0 38.3 %all-to-all-start.1 = ((bf16[64,2,8,2,128]{4,2,3,1,0:T(8,128)(2,1)}), bf16[64,2,8,2,128]{4,2,3,1,0:T(8,128)(2,1)S(1)}, u32[]{:S(2)}, u32[]{:S(2)}) async-start(bf16[64,2,8,2,128]{4,2,3,1,0:T(8,128)(2,1)} %broadcast_select_fusion.1), calls=%async_computation.1 | async-start | bytes 1048576 | tf_op jit(solution)/shard_map/all_to_all | solution.py:59
  117.3 38.3 %all-to-all-start.3 = ((bf16[64,2,8,2,128]{4,2,3,1,0:T(8,128)(2,1)}), bf16[64,2,8,2,128]{4,2,3,1,0:T(8,128)(2,1)S(1)}, u32[]{:S(2)}, u32[]{:S(2)}) async-start(bf16[64,2,8,2,128]{4,2,3,1,0:T(8,128)(2,1)} %broadcast_select_fusion), calls=%async_computation.3 | async-start | bytes 1048576 | tf_op jit(solution)/shard_map/all_to_all | solution.py:59
  155.7 55.6 %all-to-all-start.2 = ((bf16[8,8,128,2,128]{2,1,4,3,0:T(8,128)(2,1)}), bf16[8,8,128,2,128]{2,1,4,3,0:T(8,128)(2,1)}, u32[]{:S(2)}, u32[]{:S(2)}) async-start(bf16[8,8,128,2,128]{2,1,4,3,0:T(8,128)(2,1)} %fusion.29), calls=%async_computation.2 | async-start | bytes 8388608 | tf_op jit(solution)/shard_map/all_to_all | solution.py:69
  211.3 54.7 %all-to-all-start.4 = ((bf16[8,8,128,2,128]{2,1,4,3,0:T(8,128)(2,1)}), bf16[8,8,128,2,128]{2,1,4,3,0:T(8,128)(2,1)}, u32[]{:S(2)}, u32[]{:S(2)}) async-start(bf16[8,8,128,2,128]{2,1,4,3,0:T(8,128)(2,1)} %fusion.27), calls=%async_computation.4 | async-start | bytes 8388608 | tf_op jit(solution)/shard_map/all_to_all | solution.py:69
  266.0 3.4 %copy-start = (bf16[8,128,2,8,128]{1,4,3,2,0:T(8,128)(2,1)S(1)}, bf16[8,128,2,8,128]{1,4,3,2,0:T(8,128)(2,1)}, u32[]{:S(2)}) copy-start(bf16[8,128,2,8,128]{1,4,3,2,0:T(8,128)(2,1)} %copy.11) | copy-start | bytes 12582916
